TPU v7x, 32 devices: a whole 2x2x4 slice. The times are simulated.
32 devices in a mesh: row: 4 (over y, x), col: 2 (over core), depth: 4 (over z).
Axes of the slice: x: 2, y: 2, z: 4, core: 2. Of those that a mesh axis runs over, the one named last changes fastest.
Arguments:
- features: bfloat16 [8192, 128], P(('row', 'col', 'depth')), may hold values from -6 to 6
- degree: int32 [8192], P(('row', 'col', 'depth')), may hold values from 4 to 32
- tiles: bfloat16 [4, 2, 4, 256, 128, 128], P('row', 'col', 'depth'), may hold values from 0 to 1, as said below
- tile_rows: int32 [4, 2, 4, 256], P('row', 'col', 'depth'), may hold values from 0 to 3
- tile_cols: int32 [4, 2, 4, 256], P('row', 'col', 'depth'), may hold values from 0 to 31
- tile_count: int32 [4, 2, 4], P('row', 'col', 'depth'), may hold values from 32 to 256, as said below
- weight: bfloat16 [128, 256], replicated, may hold values from -0.5 to 0.5
- bias: float32 [256], replicated, may hold values from -3 to 3
- cotangent: bfloat16 [8192, 256], P(('row', 'col', 'depth')), may hold values from -6 to 6
Outputs:
- hidden: bfloat16 [8192, 256], P(('row', 'col', 'depth'))
- weight_grad: float32 [128, 256], replicated
- bias_grad: float32 [256], replicated
- input_gradient: bfloat16 [8192, 128], P(('row', 'col', 'depth'))
Inputs may be any that keep to these rules, and one draw needn't show every extreme that they name: `tile_count`: every device has 32 to 256 live slots, and some device has all 256. `tiles`: every entry is 0 or 1.
All inputs are finite; a program needn't handle non-finite values.
Results may differ from a plain program's by a relative error of at most 0.012.
Values may be sent and summed in bfloat16 or wider, within the bound.
A program may use at most 128 MiB of HBM per device.

v0:
```python
import jax
import jax.numpy as jnp
from jax import lax
from jax.sharding import PartitionSpec as P


def silu_parts(pre_act):
    sigma = jax.nn.sigmoid(pre_act)
    return (pre_act * sigma, sigma * (1.0 + pre_act * (1.0 - sigma)))


def dense_part(mixed, weight, bias, cotangent):
    pre_act = jnp.dot(mixed, weight, preferred_element_type=jnp.float32) + bias
    activated, slope_value = silu_parts(pre_act)
    hidden = activated.astype(jnp.bfloat16)
    pre_grad = (cotangent.astype(jnp.float32) * slope_value).astype(jnp.bfloat16)
    weight_part = lax.dot_general(
        mixed, pre_grad, (((0,), (0,)), ((), ())), preferred_element_type=jnp.float32
    )
    bias_portion = jnp.sum(pre_grad.astype(jnp.float32), axis=0)
    agg_grad = jnp.dot(pre_grad, weight.T, preferred_element_type=jnp.float32).astype(jnp.bfloat16)
    return (hidden, weight_part, bias_portion, agg_grad)


def local(features, degree, tiles, tile_rows, tile_cols, tile_count, weight, bias, cotangent):
    node_dev, feature_width = features.shape
    tile_size = tiles.shape[-1]
    slot_total = tiles.shape[3]
    tile_block = tiles.reshape(slot_total, tile_size, tile_size)
    rows_here = tile_rows.reshape(slot_total)
    cols_here = tile_cols.reshape(slot_total)
    live_count = tile_count.reshape(())
    col_total = lax.axis_size("col")
    row_tiles = col_total * node_dev // tile_size
    node_total = node_dev * lax.axis_size("row") * col_total * lax.axis_size("depth")
    grad_norm = node_total ** (-0.5)
    node_scale = lax.rsqrt(degree.astype(jnp.float32))[:, None]
    scaled = (features.astype(jnp.float32) * node_scale).astype(jnp.bfloat16)
    panel_rows = lax.all_gather(scaled, ("row", "depth"), axis=0, tiled=True)
    col_tiles = panel_rows.shape[0] // tile_size
    source = jnp.take(panel_rows.reshape(col_tiles, tile_size, feature_width), cols_here, axis=0)
    matmul_results = jnp.einsum(
        "tab,tbf->taf", tile_block, source, preferred_element_type=jnp.float32
    )
    is_live = jnp.arange(slot_total, dtype=jnp.int32) < live_count
    row_target = jnp.where(is_live, rows_here, row_tiles)
    partial_result = jax.ops.segment_sum(matmul_results, row_target, num_segments=row_tiles + 1)[
        :row_tiles
    ]
    partial_result = partial_result.reshape(row_tiles * tile_size, feature_width)
    aggregate = lax.psum_scatter(partial_result, "col", scatter_dimension=0, tiled=True)
    mixed = (node_scale * (aggregate + scaled.astype(jnp.float32))).astype(jnp.bfloat16)
    hidden, weight_part, bias_portion, agg_grad = dense_part(mixed, weight, bias, cotangent)
    weight_grad, bias_grad = lax.psum((weight_part, bias_portion), ("row", "col", "depth"))
    scaled_grad = (agg_grad.astype(jnp.float32) * node_scale).astype(jnp.bfloat16)
    group_grad = lax.all_gather(scaled_grad, "col", axis=0, tiled=True)
    group_sender = jnp.take(
        group_grad.reshape(row_tiles, tile_size, feature_width), rows_here, axis=0
    )
    back_products = jnp.einsum(
        "tab,taf->tbf", tile_block, group_sender, preferred_element_type=jnp.float32
    )
    count = node_dev * lax.axis_size(("row", "depth"))
    span = count // tile_size
    inside = is_live & (cols_here >= 0) & (cols_here < span)
    target = jnp.where(inside, cols_here, span)
    terms = jax.ops.segment_sum(back_products, target, num_segments=span + 1)[:span]
    back_sum = lax.psum_scatter(
        terms.reshape(count, feature_width), ("row", "depth"), scatter_dimension=0, tiled=True
    )
    input_gradient = (node_scale * (back_sum + scaled_grad.astype(jnp.float32))).astype(
        jnp.bfloat16
    )
    return (hidden, weight_grad * grad_norm, bias_grad * grad_norm, input_gradient)


def solution(mesh):
    return jax.shard_map(
        local,
        mesh=mesh,
        in_specs=(
            P(("row", "col", "depth"), None),
            P(("row", "col", "depth")),
            P("row", "col", "depth", None, None, None),
            P("row", "col", "depth", None),
            P("row", "col", "depth", None),
            P("row", "col", "depth"),
            P(),
            P(),
            P(("row", "col", "depth"), None),
        ),
        out_specs=(P(("row", "col", "depth"), None), P(), P(), P(("row", "col", "depth"), None)),
        check_vma=False,
    )
```

profile of v0, /device:TPU:0, one launch (start us, length us, event | category | flops | bytes accessed | tf_op | source)
XLA Modules:
  0.0 374.7 jit_solution(18327480170970923775)
XLA Ops:
  7.2 0.0 copy-start
  7.2 0.0 all-gather.2.cloned.1.call-start
  7.2 0.7 convert_rsqrt_fusion
  7.9 1.6 multiply_convert_fusion.4
  9.5 0.0 all-gather.2.cloned.1.call-update
  9.5 0.0 reduce-scatter.3.cloned.1.call-start
  10.2 0.7 compare_select_fusion
  10.9 0.7 compare_and_fusion.1
  11.6 57.8 %all-gather.2.cloned.1.call-done = bf16[4096,128]{1,0:T(8,128)(2,1)} async-done(((bf16[256,128]{1,0:T(8,128)(2,1)}), bf16[4096,128]{1,0:T(8,128)(2,1)}) %all-gather.2.cloned.1.call-update) | async-done | bytes 1048592 | tf_op jit(solution)/shard_map/all_gather | solution.py:39
  69.4 9.8 %gather_fusion = bf16[256,128,128]{2,1,0:T(8,128)(2,1)} fusion(bf16[32,128,128]{2,1,0:T(8,128)(2,1)} %bitcast.34, s32[1024]{0:T(1024)S(1)} %pad_clamp_fusion.1), kind=kCustom, calls=%fused_computation | custom fusion | bytes 16778240 | tf_op jit(solution)/shard_map/jit(_take)/gather | solution.py:41
  79.3 13.2 %convolution_bitcast_fusion.1 = f32[256,128,128]{1,2,0:T(8,128)} fusion(bf16[1,1,1,256,128,128]{5,4,3,2,1,0:T(8,128)(2,1)} %param.11, bf16[256,128,128]{2,1,0:T(8,128)(2,1)} %gather_fusion, pred[256]{0:T(512)(128)(4,1)S(1)} %compare_and_fusion.1), kind=kOutput, calls=%fused_computation.5 | convolution fusion | flops 1077936128 | bytes 33554688 | tf_op jit(solution)/shard_map/tab,tbf->taf/dot_general | solution.py:42
  92.4 17.5 %copy.16 = f32[256,128,128]{2,1,0:T(8,128)} copy(f32[256,128,128]{1,2,0:T(8,128)} %convolution_bitcast_fusion.1) | data formatting | bytes 33554432 | tf_op jit(solution)/shard_map/tab,tbf->taf/dot_general | solution.py:42
  109.9 0.0 copy-start.3
  109.9 0.0 copy-start.2
  109.9 0.0 copy-start.4
  110.0 0.0 copy-start.5
  110.0 33.1 %scatter_fusion = f32[5,128,128]{2,1,0:T(8,128)S(1)} fusion(f32[5,128,128]{2,1,0:T(8,128)S(1)} %broadcast_in_dim.35, s32[256]{0:T(256)S(1)} %bitcast.38, f32[256,128,128]{2,1,0:T(8,128)} %copy.16), kind=kCustom, calls=%fused_computation.2 | custom fusion | flops 4194304 | bytes 50332672 | tf_op jit(solution)/shard_map/scatter-add | solution.py:47
  143.1 0.7 slice.12
  143.8 0.0 reduce-scatter.3.cloned.1.call-update
  143.8 0.0 all-reduce.2.cloned.1.call-start
  143.9 0.0 copy-done.3
  143.9 6.5 %reduce-scatter.3.cloned.1.call-done = f32[256,128]{1,0:T(8,128)} async-done(((f32[512,128]{1,0:T(8,128)}), f32[256,128]{1,0:T(8,128)}) %reduce-scatter.3.cloned.1.call-update) | async-done | bytes 131088 | tf_op jit(solution)/shard_map/reduce_scatter | solution.py:51
  150.5 0.0 copy-done.2
  150.5 1.0 multiply_convert_fusion.3
  151.5 0.0 copy-done
  151.5 0.0 copy-done.4
  151.5 0.0 copy-done.5
  151.5 0.9 convert_reduce_fusion
  152.4 0.2 fusion.10
  152.6 0.9 fusion.13
  153.5 1.9 all_gather.7
  155.4 0.0 all-reduce.2.cloned.1.call-update
  155.4 0.2 reduce-scatter.5.cloned.1.call-start
  155.6 8.5 %gather_fusion.1 = bf16[256,128,128]{2,1,0:T(8,128)(2,1)} fusion(bf16[4,128,128]{2,1,0:T(8,128)(2,1)S(1)} %bitcast.33, s32[1024]{0:T(1024)S(1)} %pad_clamp_fusion), kind=kCustom, calls=%fused_computation.1 | custom fusion | bytes 16778240 | tf_op jit(solution)/shard_map/jit(_take)/gather | solution.py:57
  164.2 14.7 %convolution_bitcast_fusion = f32[256,128,128]{1,2,0:T(8,128)} fusion(bf16[1,1,1,256,128,128]{5,4,3,2,1,0:T(8,128)(2,1)} %param.11, bf16[256,128,128]{2,1,0:T(8,128)(2,1)} %gather_fusion.1, pred[256]{0:T(512)(128)(4,1)S(1)} %compare_and_fusion), kind=kOutput, calls=%fused_computation.4 | convolution fusion | flops 1077936128 | bytes 33554688 | tf_op jit(solution)/shard_map/tab,taf->tbf/dot_general | solution.py:60
  178.8 17.5 %copy.18 = f32[256,128,128]{2,1,0:T(8,128)} copy(f32[256,128,128]{1,2,0:T(8,128)} %convolution_bitcast_fusion) | data formatting | bytes 33554432 | tf_op jit(solution)/shard_map/tab,taf->tbf/dot_general | solution.py:60
  196.3 0.2 broadcast_in_dim.39
  196.6 0.0 copy-start.1
  196.6 33.2 %scatter_fusion.1 = f32[33,128,128]{2,1,0:T(8,128)S(1)} fusion(f32[33,128,128]{2,1,0:T(8,128)S(1)} %broadcast_in_dim.39, s32[256]{0:T(256)S(1)} %bitcast.37, f32[256,128,128]{2,1,0:T(8,128)} %copy.18), kind=kCustom, calls=%fused_computation.3 | custom fusion | flops 4194304 | bytes 50332672 | tf_op jit(solution)/shard_map/scatter-add | solution.py:67
  229.8 1.5 slice.13
  231.3 0.0 reduce-scatter.5.cloned.1.call-update
  231.4 40.4 %psum.15 = f32[256]{0:T(256)S(1)} all-reduce(f32[256]{0:T(256)S(1)} %get-tuple-element.4), channel_id=1, replica_groups=mesh['row'=4,'col'=2,'depth'=4] {'row','col','depth'}, use_global_device_ids=true, to_apply=%region_4.5 | all-reduce | flops 256 | bytes 2048 | tf_op jit(solution)/shard_map/psum | solution.py:54
  271.8 0.6 broadcast_multiply_fusion.1
  272.3 8.7 %all-reduce.2.cloned.1.call-done = f32[128,256]{1,0:T(8,128)} async-done(((f32[128,256]{1,0:T(8,128)}), f32[128,256]{1,0:T(8,128)}) %all-reduce.2.cloned.1.call-update) | async-done | bytes 131088 | tf_op jit(solution)/shard_map/psum | solution.py:54
  281.0 1.6 broadcast_multiply_fusion
  282.6 83.9 %reduce-scatter.5.cloned.1.call-done = f32[256,128]{1,0:T(8,128)} async-done(((f32[4096,128]{1,0:T(8,128)}), f32[256,128]{1,0:T(8,128)}) %reduce-scatter.5.cloned.1.call-update) | async-done | bytes 131088 | tf_op jit(solution)/shard_map/reduce_scatter | solution.py:68
  366.5 1.6 multiply_convert_fusion.2
  368.2 0.0 copy-done.1
  (4 shorter events, 0.0 us)
Async XLA Ops:
  7.2 144.3 %copy-start = (bf16[128,256]{1,0:T(8,128)(2,1)S(1)}, bf16[128,256]{1,0:T(8,128)(2,1)}, u32[]{:S(2)}) copy-start(bf16[128,256]{1,0:T(8,128)(2,1)} %param.15) | copy-start | bytes 196612
  7.2 62.2 %all-gather.2.cloned.1.call-start = ((), (), s32[]{:S(2)}) async-start(), calls=%async_computation.2 | async-start | bytes 1114112 | tf_op jit(solution)/shard_map/all_gather | solution.py:39
  9.5 140.9 %reduce-scatter.3.cloned.1.call-start = ((), (), s32[]{:S(2)}) async-start(), calls=%async_computation.3 | async-start | bytes 393216 | tf_op jit(solution)/shard_map/reduce_scatter | solution.py:51
  109.9 34.0 %copy-start.3 = (s32[1,1,1,256]{3,2,1,0:T(1,128)S(1)}, s32[1,1,1,256]{3,2,1,0:T(1,128)}, u32[]{:S(2)}) copy-start(s32[1,1,1,256]{3,2,1,0:T(1,128)} %param.12) | copy-start | bytes 3076
  109.9 40.5 %copy-start.2 = (bf16[256,128]{1,0:T(8,128)(2,1)S(1)}, bf16[256,128]{1,0:T(8,128)(2,1)}, u32[]{:S(2)}) copy-start(bf16[256,128]{1,0:T(8,128)(2,1)} %param.9) | copy-start | bytes 196612
  109.9 41.5 %copy-start.4 = (bf16[256,256]{1,0:T(8,128)(2,1)S(1)}, bf16[256,256]{1,0:T(8,128)(2,1)}, u32[]{:S(2)}) copy-start(bf16[256,256]{1,0:T(8,128)(2,1)} %param.17) | copy-start | bytes 393220
  110.0 41.5 %copy-start.5 = (f32[256]{0:T(256)S(1)}, f32[256]{0:T(256)}, u32[]{:S(2)}) copy-start(f32[256]{0:T(256)} %param.16) | copy-start | bytes 3076
  143.8 137.2 %all-reduce.2.cloned.1.call-start = ((), (), s32[]{:S(2)}) async-start(), calls=%async_computation.4 | async-start | bytes 262144 | tf_op jit(solution)/shard_map/psum | solution.py:54
  155.4 211.1 %reduce-scatter.5.cloned.1.call-start = ((), (), s32[]{:S(2)}) async-start(), calls=%async_computation.5 | async-start | bytes 2228224 | tf_op jit(solution)/shard_map/reduce_scatter | solution.py:68
  196.6 171.6 %copy-start.1 = (bf16[128,256]{1,0:T(8,128)(2,1)S(1)}, bf16[128,256]{1,0:T(8,128)(2,1)}, u32[]{:S(2)}) copy-start(bf16[128,256]{1,0:T(8,128)(2,1)} %param.15) | copy-start | bytes 196612
Sparse Core Ops, SparseCore 0:
  11.3 58.0 all-gather.1
  143.9 6.4 reduce-scatter.2
  157.5 123.5 all-reduce.1
  283.3 83.2 reduce-scatter.4
where the time goes:
time: 377 us; the launch traced here: 375 us
  waiting for transfers between devices  157 us (42%)
  other arithmetic  74.8 us (20%)
  local copies, waits for them, and re-layouts  55.8 us (15%)
  blocking collectives  42.3 us (11%)
  matrix products  29.8 us (8%)
  between operations  14.6 us (4%)
    reduce_scatter x1, waiting for transfers between devices, local(): lax.psum_scatter(terms.reshape(count, feature_width), ('row', 'depth'), s...  83.9 us
    all_gather x1, waiting for transfers between devices, local(): panel_rows = lax.all_gather(scaled, ('row', 'depth'), axis=0, tiled=True)  57.8 us
    psum x1, blocking collectives, local(): lax.psum((weight_part, bias_portion), ('row', 'col', 'depth'))  40.4 us
    scatter-add x1, other arithmetic, local(): jax.ops.segment_sum(back_products, target, num_segments=span + 1)[:span]  33.2 us
    scatter-add x1, other arithmetic, local(): jax.ops.segment_sum(matmul_results, row_target, num_segments=row_tiles + 1)  33.1 us
    dot_general x1, local copies, waits for them, and re-layouts, local(): jnp.einsum('tab,taf->tbf', tile_block, group_sender, preferred_element_ty...  17.5 us
    dot_general x1, local copies, waits for them, and re-layouts, local(): jnp.einsum('tab,tbf->taf', tile_block, source, preferred_element_type=jnp...  17.5 us
    dot_general x1, matrix products, local(): jnp.einsum('tab,taf->tbf', tile_block, group_sender, preferred_element_ty...  14.7 us
  transfers between devices with their start and end apart: 4, of which 4 were waited for; matrix products, arithmetic and copies ran while one was open for 21% of the time, Pallas kernels for 0%

commit v1 on v0

v1 whole, which is shorter than its diff:
```python
import functools

import jax
import jax.numpy as jnp
from jax import lax
from jax.experimental import pallas as pl
from jax.experimental.pallas import tpu as pltpu
from jax.sharding import PartitionSpec as P


def build_kernel(chunk, rows_ref, cols_ref, count_ref, tiles_ref, out_ref, held, sems):
    slots, tile, _ = held.shape
    live = count_ref[0]

    def fetch(k):
        part = pl.ds(k * chunk, chunk)
        return pltpu.make_async_copy(tiles_ref.at[part], held.at[part], sems.at[k])

    for k in range(slots // chunk):

        @pl.when(k * chunk < live)
        def _():
            fetch(k).start()

    zero = jnp.zeros((16, out_ref.shape[1]), out_ref.dtype)

    def clear(i, carry):
        out_ref[pl.ds(pl.multiple_of(i * 16, 16), 16), :] = zero
        return carry

    lax.fori_loop(0, out_ref.shape[0] // 16, clear, 0)

    def add(t, carry):
        at = (
            pl.ds(pl.multiple_of(rows_ref[t] * tile, tile), tile),
            pl.ds(pl.multiple_of(cols_ref[t] * tile, tile), tile),
        )
        out_ref[at] = out_ref[at] + held[t]
        return carry

    for k in range(slots // chunk):

        @pl.when(k * chunk < live)
        def _():
            fetch(k).wait()
            lax.fori_loop(k * chunk, jnp.minimum((k + 1) * chunk, live), add, 0)


def build_block(tiles, rows, cols, count, row_tiles, col_tiles):
    slots, tile, _ = tiles.shape
    chunk = 32
    shape = (row_tiles * tile, col_tiles * tile)
    smem = pl.BlockSpec(memory_space=pltpu.SMEM)
    return pl.pallas_call(
        functools.partial(build_kernel, chunk),
        out_shape=jax.ShapeDtypeStruct(shape, jnp.bfloat16),
        in_specs=[smem, smem, smem, pl.BlockSpec(memory_space=pl.ANY)],
        out_specs=pl.BlockSpec(memory_space=pltpu.VMEM),
        scratch_shapes=[
            pltpu.VMEM(tiles.shape, tiles.dtype),
            pltpu.SemaphoreType.DMA((slots // chunk,)),
        ],
        compiler_params=pltpu.CompilerParams(vmem_limit_bytes=56 * 1024 * 1024),
        cost_estimate=pl.CostEstimate(
            flops=tiles.size, bytes_accessed=tiles.size * 2 + shape[0] * shape[1] * 2, transcendentals=0
        ),
    )(rows, cols, count, tiles)


def silu_parts(pre_act):
    sigma = jax.nn.sigmoid(pre_act)
    return (pre_act * sigma, sigma * (1.0 + pre_act * (1.0 - sigma)))


def dense_part(mixed, weight, bias, cotangent):
    pre_act = jnp.dot(mixed, weight, preferred_element_type=jnp.float32) + bias
    activated, slope_value = silu_parts(pre_act)
    hidden = activated.astype(jnp.bfloat16)
    pre_grad = (cotangent.astype(jnp.float32) * slope_value).astype(jnp.bfloat16)
    weight_part = lax.dot_general(
        mixed, pre_grad, (((0,), (0,)), ((), ())), preferred_element_type=jnp.float32
    )
    bias_portion = jnp.sum(pre_grad.astype(jnp.float32), axis=0)
    agg_grad = jnp.dot(pre_grad, weight.T, preferred_element_type=jnp.float32).astype(jnp.bfloat16)
    return (hidden, weight_part, bias_portion, agg_grad)


def local(features, degree, tiles, tile_rows, tile_cols, tile_count, weight, bias, cotangent):
    node_dev, feature_width = features.shape
    tile_size = tiles.shape[-1]
    slot_total = tiles.shape[3]
    col_total = lax.axis_size("col")
    row_tiles = col_total * node_dev // tile_size
    span = lax.axis_size(("row", "depth")) * node_dev // tile_size
    node_total = node_dev * lax.axis_size(("row", "col", "depth"))
    grad_norm = node_total ** (-0.5)
    node_scale = lax.rsqrt(degree.astype(jnp.float32))[:, None]
    scaled = (features.astype(jnp.float32) * node_scale).astype(jnp.bfloat16)
    panel_rows = lax.all_gather(scaled, ("row", "depth"), axis=0, tiled=True)
    block = build_block(
        tiles.reshape(slot_total, tile_size, tile_size),
        tile_rows.reshape(slot_total),
        tile_cols.reshape(slot_total),
        tile_count.reshape(1),
        row_tiles,
        span,
    )
    partial_result = jnp.dot(block, panel_rows, preferred_element_type=jnp.float32)
    aggregate = lax.psum_scatter(partial_result, "col", scatter_dimension=0, tiled=True)
    mixed = (node_scale * (aggregate + scaled.astype(jnp.float32))).astype(jnp.bfloat16)
    hidden, weight_part, bias_portion, agg_grad = dense_part(mixed, weight, bias, cotangent)
    weight_grad, bias_grad = lax.psum((weight_part, bias_portion), ("row", "col", "depth"))
    scaled_grad = (agg_grad.astype(jnp.float32) * node_scale).astype(jnp.bfloat16)
    group_grad = lax.all_gather(scaled_grad, "col", axis=0, tiled=True)
    terms = lax.dot_general(
        block, group_grad, (((0,), (0,)), ((), ())), preferred_element_type=jnp.float32
    )
    back_sum = lax.psum_scatter(terms, ("row", "depth"), scatter_dimension=0, tiled=True)
    input_gradient = (node_scale * (back_sum + scaled_grad.astype(jnp.float32))).astype(
        jnp.bfloat16
    )
    return (hidden, weight_grad * grad_norm, bias_grad * grad_norm, input_gradient)


def solution(mesh):
    return jax.shard_map(
        local,
        mesh=mesh,
        in_specs=(
            P(("row", "col", "depth"), None),
            P(("row", "col", "depth")),
            P("row", "col", "depth", None, None, None),
            P("row", "col", "depth", None),
            P("row", "col", "depth", None),
            P("row", "col", "depth"),
            P(),
            P(),
            P(("row", "col", "depth"), None),
        ),
        out_specs=(P(("row", "col", "depth"), None), P(), P(), P(("row", "col", "depth"), None)),
        check_vma=False,
    )
```

time: 377 us -> 305 us (0.81)
  other arithmetic: 74.8 us -> 7.03 us
  waiting for transfers between devices: 157 us -> 222 us
  local copies, waits for them, and re-layouts: 55.8 us -> 0.03 us
  matrix products: 29.8 us -> 11.2 us
  Pallas kernels: 0 us -> 7.46 us
    psum x1, waiting for transfers between devices: 8.71 us -> 79.8 us  [local(): lax.psum((weight_part, bias_portion), ('row', 'col', 'depth'))]
    scatter-add x2 -> x0, other arithmetic: 66.4 us -> none  [the longest x1 33.2 us: local(): jax.ops.segment_sum(back_products, target, num_segments=span + 1)[:span]]
    dot_general x2 -> x0, local copies, waits for them, and re-layouts: 34.9 us -> none  [the longest x1 17.5 us: local(): jnp.einsum('tab,taf->tbf', tile_block, group_sender, preferred_element_ty...]
    dot_general x2, matrix products: 27.9 us -> 9.23 us  [the longest x1 4.79 us: local(): lax.dot_general(block, group_grad, (((0,), (0,)), ((), ())), preferred_el...]
    gather x2 -> x0, local copies, waits for them, and re-layouts: 18.4 us -> none  [the longest x1 9.83 us: local(): jnp.take(panel_rows.reshape(col_tiles, tile_size, feature_width), cols_he...]
    pallas_call x0 -> x1, Pallas kernels: none -> 7.46 us  [build_block(): pl.pallas_call(functools.partial(build_kernel, chunk), out_shape=jax.Shap...]
    all_gather x1, waiting for transfers between devices: 57.8 us -> 51.7 us  [local(): panel_rows = lax.all_gather(scaled, ('row', 'depth'), axis=0, tiled=True)]
  transfers between devices with their start and end apart: 4 -> 4, of which waited for: 4 -> 4; matrix products, arithmetic and copies ran while one was open for 21% -> 2% of each run, Pallas kernels for 0% -> 2%
where the time goes in v1:
time: 305 us
  waiting for transfers between devices  222 us (73%)
  blocking collectives  42.4 us (14%)
  between operations  14.5 us (5%)
  matrix products  11.2 us (4%)
  Pallas kernels  7.46 us (2%)
  other arithmetic  7.03 us (2%)
    reduce_scatter x1, waiting for transfers between devices, local(): lax.psum_scatter(terms, ('row', 'depth'), scatter_dimension=0, tiled=True)  83.9 us
    psum x1, waiting for transfers between devices, local(): lax.psum((weight_part, bias_portion), ('row', 'col', 'depth'))  79.8 us
    all_gather x1, waiting for transfers between devices, local(): panel_rows = lax.all_gather(scaled, ('row', 'depth'), axis=0, tiled=True)  51.7 us
    psum x1, blocking collectives, local(): lax.psum((weight_part, bias_portion), ('row', 'col', 'depth'))  40.5 us
    pallas_call x1, Pallas kernels, build_block(): pl.pallas_call(functools.partial(build_kernel, chunk), out_shape=jax.Shap...  7.46 us
    reduce_scatter x1, waiting for transfers between devices, local(): lax.psum_scatter(partial_result, 'col', scatter_dimension=0, tiled=True)  6.58 us
  transfers between devices with their start and end apart: 4, of which 4 were waited for; matrix products, arithmetic and copies ran while one was open for 2% of the time, Pallas kernels for 2%

profile of v1, /device:TPU:0, one launch (start us, length us, event | category | flops | bytes accessed | tf_op | source)
XLA Modules:
  0.0 304.9 jit_solution(12349685272395525871)
XLA Ops:
  7.2 0.0 copy-start
  7.2 0.0 all-gather.2.cloned.1.call-start
  7.2 0.7 convert_rsqrt_fusion
  7.9 1.6 multiply_convert_fusion.4
  9.5 0.0 all-gather.2.cloned.1.call-update
  9.5 0.0 reduce-scatter.3.cloned.1.call-start
  10.2 7.5 %shard_map.120 = bf16[512,4096]{1,0:T(8,128)(2,1)} custom-call(s32[256]{0:T(256)} %bitcast.16, s32[256]{0:T(256)} %bitcast.17, s32[1]{0:T(128)} %bitcast.14.count_ref, bf16[256,128,128]{2,1,0:T(8,128)(2,1)} %bitcast.15), custom_call_target="tpu_custom_call" | custom-call | flops 4194304 | bytes 12582912 | tf_op jit(solution)/shard_map/pallas_call | solution.py:54
  17.7 0.0 copy-start.1
  17.7 0.0 copy-start.2
  17.7 0.0 copy-start.3
  17.7 51.7 %all-gather.2.cloned.1.call-done = bf16[4096,128]{1,0:T(8,128)(2,1)} async-done(((bf16[256,128]{1,0:T(8,128)(2,1)}), bf16[4096,128]{1,0:T(8,128)(2,1)}) %all-gather.2.cloned.1.call-update) | async-done | bytes 1048592 | tf_op jit(solution)/shard_map/all_gather | solution.py:99
  69.4 4.4 %fusion.3 = f32[512,128]{1,0:T(8,128)} fusion(bf16[512,4096]{1,0:T(8,128)(2,1)} %shard_map.120, bf16[4096,128]{1,0:T(8,128)(2,1)} %all-gather.2.cloned.1.call-done), kind=kOutput, calls=%fused_computation.15 | convolution fusion | flops 536870912 | bytes 5505024 | tf_op jit(solution)/shard_map/dot_general | solution.py:108
  73.9 0.0 reduce-scatter.3.cloned.1.call-update
  73.9 0.0 all-reduce.2.cloned.1.call-start
  73.9 6.6 %reduce-scatter.3.cloned.1.call-done = f32[256,128]{1,0:T(8,128)} async-done(((f32[512,128]{1,0:T(8,128)}), f32[256,128]{1,0:T(8,128)}) %reduce-scatter.3.cloned.1.call-update) | async-done | bytes 131088 | tf_op jit(solution)/shard_map/reduce_scatter | solution.py:109
  80.5 0.0 copy-done.1
  80.5 1.0 multiply_convert_fusion.3
  81.5 0.0 copy-done
  81.5 0.0 copy-done.2
  81.6 0.0 copy-done.3
  81.6 0.9 convert_reduce_fusion
  82.5 0.2 fusion.2
  82.7 0.9 fusion.4
  83.6 0.0 all-reduce.2.cloned.1.call-update
  83.6 0.0 reduce-scatter.5.cloned.1.call-start
  83.6 1.9 all_gather.7
  85.5 4.8 %fusion.5 = f32[4096,128]{1,0:T(8,128)} fusion(bf16[512,4096]{1,0:T(8,128)(2,1)} %shard_map.120, bf16[512,128]{1,0:T(8,128)(2,1)S(1)} %all_gather.7), kind=kOutput, calls=%fused_computation.17 | convolution fusion | flops 536870912 | bytes 6422528 | tf_op jit(solution)/shard_map/dot_general | solution.py:115
  90.3 0.0 reduce-scatter.5.cloned.1.call-update
  90.3 40.5 %psum.15 = f32[256]{0:T(256)S(1)} all-reduce(f32[256]{0:T(256)S(1)} %get-tuple-element.4), channel_id=1, replica_groups=mesh['row'=4,'col'=2,'depth'=4] {'row','col','depth'}, use_global_device_ids=true, to_apply=%region_3.0 | all-reduce | flops 256 | bytes 2048 | tf_op jit(solution)/shard_map/psum | solution.py:112
  130.8 0.6 broadcast_multiply_fusion.1
  131.4 79.8 %all-reduce.2.cloned.1.call-done = f32[128,256]{1,0:T(8,128)} async-done(((f32[128,256]{1,0:T(8,128)}), f32[128,256]{1,0:T(8,128)}) %all-reduce.2.cloned.1.call-update) | async-done | bytes 131088 | tf_op jit(solution)/shard_map/psum | solution.py:112
  211.2 1.6 broadcast_multiply_fusion
  212.8 83.9 %reduce-scatter.5.cloned.1.call-done = f32[256,128]{1,0:T(8,128)} async-done(((f32[4096,128]{1,0:T(8,128)}), f32[256,128]{1,0:T(8,128)}) %reduce-scatter.5.cloned.1.call-update) | async-done | bytes 131088 | tf_op jit(solution)/shard_map/reduce_scatter | solution.py:118
  296.7 1.6 multiply_convert_fusion.2
Async XLA Ops:
  7.2 74.4 %copy-start = (bf16[128,256]{1,0:T(8,128)(2,1)S(1)}, bf16[128,256]{1,0:T(8,128)(2,1)}, u32[]{:S(2)}) copy-start(bf16[128,256]{1,0:T(8,128)(2,1)} %param.15) | copy-start | bytes 196612
  7.2 62.2 %all-gather.2.cloned.1.call-start = ((), (), s32[]{:S(2)}) async-start(), calls=%async_computation.2 | async-start | bytes 1114112 | tf_op jit(solution)/shard_map/all_gather | solution.py:99
  9.5 71.0 %reduce-scatter.3.cloned.1.call-start = ((), (), s32[]{:S(2)}) async-start(), calls=%async_computation.3 | async-start | bytes 393216 | tf_op jit(solution)/shard_map/reduce_scatter | solution.py:109
  17.7 62.9 %copy-start.1 = (bf16[256,128]{1,0:T(8,128)(2,1)S(1)}, bf16[256,128]{1,0:T(8,128)(2,1)}, u32[]{:S(2)}) copy-start(bf16[256,128]{1,0:T(8,128)(2,1)} %param.9) | copy-start | bytes 196612
  17.7 63.9 %copy-start.2 = (bf16[256,256]{1,0:T(8,128)(2,1)S(1)}, bf16[256,256]{1,0:T(8,128)(2,1)}, u32[]{:S(2)}) copy-start(bf16[256,256]{1,0:T(8,128)(2,1)} %param.17) | copy-start | bytes 393220
  17.7 63.9 %copy-start.3 = (f32[256]{0:T(256)S(1)}, f32[256]{0:T(256)}, u32[]{:S(2)}) copy-start(f32[256]{0:T(256)} %param.16) | copy-start | bytes 3076
  73.9 137.3 %all-reduce.2.cloned.1.call-start = ((), (), s32[]{:S(2)}) async-start(), calls=%async_computation.4 | async-start | bytes 262144 | tf_op jit(solution)/shard_map/psum | solution.py:112
  83.6 213.1 %reduce-scatter.5.cloned.1.call-start = ((), (), s32[]{:S(2)}) async-start(), calls=%async_computation.5 | async-start | bytes 2228224 | tf_op jit(solution)/shard_map/reduce_scatter | solution.py:118
Sparse Core Ops, SparseCore 0:
  11.3 58.0 all-gather.1
  74.0 6.4 reduce-scatter.2
  87.6 123.6 all-reduce.1
  213.4 83.2 reduce-scatter.4

commit v2 on v1

--- a/solution.py
+++ b/solution.py
@@ -72,31 +72,298 @@
     return (pre_act * sigma, sigma * (1.0 + pre_act * (1.0 - sigma)))
 
 
-def dense_part(mixed, weight, bias, cotangent):
-    pre_act = jnp.dot(mixed, weight, preferred_element_type=jnp.float32) + bias
+def layer_kernel(
+    sizes,
+    grad_norm,
+    block,
+    features,
+    scale,
+    weight,
+    bias,
+    cotangent,
+    hidden,
+    weight_grad,
+    bias_grad,
+    input_gradient,
+    panel,
+    acc,
+    share,
+    grads,
+    back_own,
+    back_send,
+    back_row,
+    deep_send,
+    deep_recv,
+    w_send,
+    w_col,
+    w_row,
+    w_deep,
+    w_out,
+    panel_s,
+    panel_r,
+    share_s,
+    share_r,
+    grads_s,
+    grads_r,
+    back_s,
+    back_r,
+    deep_s,
+    deep_r,
+    wc_s,
+    wc_r,
+    wr_s,
+    wr_r,
+    wd_s,
+    wd_r,
+    wo_s,
+    wo_r,
+):
+    rows, cols, depths = sizes
+    nodes = features.shape[0]
+    me_r, me_c, me_d = (lax.axis_index(name) for name in ("row", "col", "depth"))
+    f32, bf16 = jnp.float32, jnp.bfloat16
+
+    def row_of(j):
+        return lax.rem(me_r + j, rows)
+
+    def col_of(m):
+        return lax.rem(me_c + m, cols)
+
+    def deep_of(k):
+        return lax.rem(me_d + k, depths)
+
+    def send(src, dst, send_sem, recv_sem, **peer):
+        return pltpu.make_async_remote_copy(
+            src_ref=src,
+            dst_ref=dst,
+            send_sem=send_sem,
+            recv_sem=recv_sem,
+            device_id=peer,
+            device_id_type=pl.DeviceIdType.MESH,
+        )
+
+    sent = []
+
+    def start(*args, **peer):
+        copy = send(*args, **peer)
+        copy.start()
+        sent.append(copy)
+
+    deep_order = sorted(range(1, depths), key=lambda k: (min(k, depths - k), k))
+
+    barrier = pltpu.get_barrier_semaphore()
+    for m in range(1, cols):
+        pl.semaphore_signal(barrier, inc=1, device_id={"col": col_of(m)}, device_id_type=pl.DeviceIdType.MESH)
+    for j in range(1, rows):
+        pl.semaphore_signal(barrier, inc=1, device_id={"row": row_of(j)}, device_id_type=pl.DeviceIdType.MESH)
+    for k in range(1, depths):
+        pl.semaphore_signal(barrier, inc=1, device_id={"depth": deep_of(k)}, device_id_type=pl.DeviceIdType.MESH)
+    mine = me_r * depths + me_d
+    scaled = (features[...].astype(f32) * scale[...]).astype(bf16)
+    panel[mine] = scaled
+    pl.semaphore_wait(barrier, cols + rows + depths - 3)
+
+    for k in deep_order:
+        start(panel.at[mine], panel.at[mine], panel_s.at[k, 0], panel_r.at[mine], depth=deep_of(k))
+    for j in range(1, rows):
+        start(panel.at[mine], panel.at[mine], panel_s.at[0, j], panel_r.at[mine], row=row_of(j))
+
+    def product(q):
+        at = pl.ds(pl.multiple_of(q * nodes, nodes), nodes)
+        return jnp.dot(block[:, at], panel[q], preferred_element_type=f32)
+
+    acc[...] = product(mine)
+    for k in deep_order:
+        q = me_r * depths + deep_of(k)
+        send(panel.at[q], panel.at[q], panel_s.at[k, 0], panel_r.at[q], depth=deep_of(k)).wait_recv()
+        for j in range(1, rows):
+            start(panel.at[q], panel.at[q], panel_s.at[k, j], panel_r.at[q], row=row_of(j))
+        acc[...] += product(q)
+    for k in [0] + deep_order:
+        for j in range(1, rows):
+            q = row_of(j) * depths + deep_of(k)
+            send(panel.at[q], panel.at[q], panel_s.at[k, j], panel_r.at[q], row=row_of(j)).wait_recv()
+            acc[...] += product(q)
+
+    def acc_of(c):
+        return acc.at[pl.ds(pl.multiple_of(c * nodes, nodes), nodes)]
+
+    for m in range(1, cols):
+        start(acc_of(col_of(m)), share.at[m - 1], share_s.at[m - 1], share_r.at[m - 1], col=col_of(m))
+    aggregate = acc_of(me_c)[...]
+    for m in range(1, cols):
+        send(acc_of(me_c), share.at[m - 1], share_s.at[m - 1], share_r.at[m - 1], col=col_of(m)).wait_recv()
+        aggregate = aggregate + share[m - 1]
+
+    mixed = (scale[...] * (aggregate + scaled.astype(f32))).astype(bf16)
+    pre_act = jnp.dot(mixed, weight[...], preferred_element_type=f32) + bias[...]
     activated, slope_value = silu_parts(pre_act)
-    hidden = activated.astype(jnp.bfloat16)
-    pre_grad = (cotangent.astype(jnp.float32) * slope_value).astype(jnp.bfloat16)
-    weight_part = lax.dot_general(
-        mixed, pre_grad, (((0,), (0,)), ((), ())), preferred_element_type=jnp.float32
-    )
-    bias_portion = jnp.sum(pre_grad.astype(jnp.float32), axis=0)
-    agg_grad = jnp.dot(pre_grad, weight.T, preferred_element_type=jnp.float32).astype(jnp.bfloat16)
-    return (hidden, weight_part, bias_portion, agg_grad)
+    hidden[...] = activated.astype(bf16)
+    pre_grad = (cotangent[...].astype(f32) * slope_value).astype(bf16)
+    agg_grad = lax.dot_general(
+        pre_grad, weight[...], (((1,), (1,)), ((), ())), preferred_element_type=f32
+    ).astype(bf16)
+    scaled_grad = (agg_grad.astype(f32) * scale[...]).astype(bf16)
+    grads[me_c] = scaled_grad
+    for m in range(1, cols):
+        start(grads.at[me_c], grads.at[me_c], grads_s.at[m - 1], grads_r.at[m - 1], col=col_of(m))
+
+    w_part = lax.dot_general(mixed, pre_grad, (((0,), (0,)), ((), ())), preferred_element_type=f32)
+    b_part = jnp.sum(pre_grad.astype(f32).reshape(nodes // 8, 8, pre_grad.shape[1]), axis=0)
+    band = w_part.shape[0] // cols
+    for c in range(cols):
+        w_send[c, :band] = w_part[c * band : (c + 1) * band]
+        w_send[c, band:] = b_part
+    for m in range(1, cols):
+        start(w_send.at[col_of(m)], w_col.at[me_c], wc_s.at[m - 1], wc_r.at[m - 1], col=col_of(m))
+    w_col[me_c] = w_send[me_c]
+
+    for m in range(1, cols):
+        c = lax.rem(me_c + cols - m, cols)
+        send(grads.at[c], grads.at[c], grads_s.at[m - 1], grads_r.at[m - 1], col=col_of(m)).wait_recv()
+    turned = grads[...].reshape(cols * nodes, scaled_grad.shape[1]).T
+
+    for k in deep_order + [0]:
+        for j in list(range(1, rows)) + [0]:
+            q = row_of(j) * depths + deep_of(k)
+            at = pl.ds(pl.multiple_of(q * nodes, nodes), nodes)
+            term = jnp.dot(turned, block[:, at], preferred_element_type=f32)
+            if j == 0:
+                back_own[k] = term
+            else:
+                back_send[k, j - 1] = term.astype(bf16)
+                start(
+                    back_send.at[k, j - 1],
+                    back_row.at[k, j - 1],
+                    back_s.at[k, j - 1],
+                    back_r.at[k, j - 1],
+                    row=row_of(j),
+                )
+
+    def total(buffer, count):
+        value = buffer[0]
+        for i in range(1, count):
+            value = value + buffer[i]
+        return value
+
+    for m in range(1, cols):
+        send(w_send.at[me_c], w_col.at[me_c], wc_s.at[m - 1], wc_r.at[m - 1], col=col_of(m)).wait_recv()
+    w_row[me_r] = total(w_col, cols)
+    for j in range(1, rows):
+        start(w_row.at[me_r], w_row.at[me_r], wr_s.at[j - 1], wr_r.at[j - 1], row=row_of(j))
+
+    def row_sum(k):
+        value = back_own[k]
+        for j in range(1, rows):
+            send(
+                back_send.at[k, j - 1],
+                back_row.at[k, j - 1],
+                back_s.at[k, j - 1],
+                back_r.at[k, j - 1],
+                row=row_of(j),
+            ).wait_recv()
+            value = value + back_row[k, j - 1].astype(f32)
+        return value
+
+    for k in deep_order:
+        deep_send[k - 1] = row_sum(k).astype(bf16)
+        start(deep_send.at[k - 1], deep_recv.at[k - 1], deep_s.at[k - 1], deep_r.at[k - 1], depth=deep_of(k))
+
+    for j in range(1, rows):
+        send(w_row.at[me_r], w_row.at[row_of(rows - j)], wr_s.at[j - 1], wr_r.at[j - 1], row=row_of(j)).wait_recv()
+    w_deep[me_d] = total(w_row, rows)
+    for k in range(1, depths):
+        start(w_deep.at[me_d], w_deep.at[me_d], wd_s.at[k - 1], wd_r.at[k - 1], depth=deep_of(k))
+
+    back = row_sum(0)
+
+    for k in range(1, depths):
+        send(
+            w_deep.at[me_d], w_deep.at[deep_of(depths - k)], wd_s.at[k - 1], wd_r.at[k - 1], depth=deep_of(k)
+        ).wait_recv()
+    w_total = total(w_deep, depths) * grad_norm
+    w_out[me_c] = w_total[:band]
+    bias_grad[...] = jnp.sum(w_total[band:], axis=0, keepdims=True)
+    for m in range(1, cols):
+        start(w_out.at[me_c], w_out.at[me_c], wo_s.at[m - 1], wo_r.at[m - 1], col=col_of(m))
+
+    for k in range(1, depths):
+        send(
+            deep_send.at[k - 1], deep_recv.at[k - 1], deep_s.at[k - 1], deep_r.at[k - 1], depth=deep_of(k)
+        ).wait_recv()
+        back = back + deep_recv[k - 1].astype(f32)
+    input_gradient[...] = (scale[...] * (back.T + grads[me_c].astype(f32))).astype(bf16)
+
+    for m in range(1, cols):
+        c = lax.rem(me_c + cols - m, cols)
+        send(w_out.at[c], w_out.at[c], wo_s.at[m - 1], wo_r.at[m - 1], col=col_of(m)).wait_recv()
+    for c in range(cols):
+        weight_grad[c * band : (c + 1) * band] = w_out[c]
+    for copy in sent:
+        copy.wait_send()
+
+
+def run_layer(sizes, grad_norm, block, features, scale, weight, bias, cotangent):
+    rows, cols, depths = sizes
+    nodes, width = features.shape
+    wide = weight.shape[1]
+    band = width // cols
+    f32, bf16 = jnp.float32, jnp.bfloat16
+
+    def dma(*shape):
+        return [pltpu.SemaphoreType.DMA(shape)] * 2
+
+    return pl.pallas_call(
+        functools.partial(layer_kernel, sizes, grad_norm),
+        out_shape=(
+            jax.ShapeDtypeStruct((nodes, wide), bf16),
+            jax.ShapeDtypeStruct((width, wide), f32),
+            jax.ShapeDtypeStruct((1, wide), f32),
+            jax.ShapeDtypeStruct((nodes, width), bf16),
+        ),
+        in_specs=[pl.BlockSpec(memory_space=pltpu.VMEM)] * 6,
+        out_specs=(pl.BlockSpec(memory_space=pltpu.VMEM),) * 4,
+        scratch_shapes=[
+            pltpu.VMEM((rows * depths, nodes, width), bf16),
+            pltpu.VMEM((cols * nodes, width), f32),
+            pltpu.VMEM((cols - 1, nodes, width), f32),
+            pltpu.VMEM((cols, nodes, width), bf16),
+            pltpu.VMEM((depths, width, nodes), f32),
+            pltpu.VMEM((depths, rows - 1, width, nodes), bf16),
+            pltpu.VMEM((depths, rows - 1, width, nodes), bf16),
+            pltpu.VMEM((depths - 1, width, nodes), bf16),
+            pltpu.VMEM((depths - 1, width, nodes), bf16),
+            pltpu.VMEM((cols, band + 8, wide), f32),
+            pltpu.VMEM((cols, band + 8, wide), f32),
+            pltpu.VMEM((rows, band + 8, wide), f32),
+            pltpu.VMEM((depths, band + 8, wide), f32),
+            pltpu.VMEM((cols, band, wide), f32),
+            pltpu.SemaphoreType.DMA((depths, rows)),
+            pltpu.SemaphoreType.DMA((rows * depths,)),
+            *dma(cols - 1),
+            *dma(cols - 1),
+            *dma(depths, rows - 1),
+            *dma(depths - 1),
+            *dma(cols - 1),
+            *dma(rows - 1),
+            *dma(depths - 1),
+            *dma(cols - 1),
+        ],
+        compiler_params=pltpu.CompilerParams(
+            collective_id=0, has_side_effects=True, vmem_limit_bytes=56 * 1024 * 1024
+        ),
+    )(block, features, scale, weight, bias, cotangent)
 
 
 def local(features, degree, tiles, tile_rows, tile_cols, tile_count, weight, bias, cotangent):
     node_dev, feature_width = features.shape
     tile_size = tiles.shape[-1]
     slot_total = tiles.shape[3]
-    col_total = lax.axis_size("col")
-    row_tiles = col_total * node_dev // tile_size
-    span = lax.axis_size(("row", "depth")) * node_dev // tile_size
-    node_total = node_dev * lax.axis_size(("row", "col", "depth"))
-    grad_norm = node_total ** (-0.5)
-    node_scale = lax.rsqrt(degree.astype(jnp.float32))[:, None]
-    scaled = (features.astype(jnp.float32) * node_scale).astype(jnp.bfloat16)
-    panel_rows = lax.all_gather(scaled, ("row", "depth"), axis=0, tiled=True)
+    sizes = tuple(lax.axis_size(name) for name in ("row", "col", "depth"))
+    row_tiles = sizes[1] * node_dev // tile_size
+    span = sizes[0] * sizes[2] * node_dev // tile_size
+    grad_norm = (node_dev * sizes[0] * sizes[1] * sizes[2]) ** (-0.5)
+    scale = jnp.broadcast_to(lax.rsqrt(degree.astype(jnp.float32))[:, None], features.shape)
     block = build_block(
         tiles.reshape(slot_total, tile_size, tile_size),
         tile_rows.reshape(slot_total),
@@ -105,21 +372,10 @@
         row_tiles,
         span,
     )
-    partial_result = jnp.dot(block, panel_rows, preferred_element_type=jnp.float32)
-    aggregate = lax.psum_scatter(partial_result, "col", scatter_dimension=0, tiled=True)
-    mixed = (node_scale * (aggregate + scaled.astype(jnp.float32))).astype(jnp.bfloat16)
-    hidden, weight_part, bias_portion, agg_grad = dense_part(mixed, weight, bias, cotangent)
-    weight_grad, bias_grad = lax.psum((weight_part, bias_portion), ("row", "col", "depth"))
-    scaled_grad = (agg_grad.astype(jnp.float32) * node_scale).astype(jnp.bfloat16)
-    group_grad = lax.all_gather(scaled_grad, "col", axis=0, tiled=True)
-    terms = lax.dot_general(
-        block, group_grad, (((0,), (0,)), ((), ())), preferred_element_type=jnp.float32
+    hidden, weight_grad, bias_grad, input_gradient = run_layer(
+        sizes, grad_norm, block, features, scale, weight, bias.reshape(1, -1), cotangent
     )
-    back_sum = lax.psum_scatter(terms, ("row", "depth"), scatter_dimension=0, tiled=True)
-    input_gradient = (node_scale * (back_sum + scaled_grad.astype(jnp.float32))).astype(
-        jnp.bfloat16
-    )
-    return (hidden, weight_grad * grad_norm, bias_grad * grad_norm, input_gradient)
+    return (hidden, weight_grad, bias_grad.reshape(-1), input_gradient)
 
 
 def solution(mesh):

time: 305 us -> 66.4 us (0.22)
  waiting for transfers between devices: 222 us -> 0 us
  Pallas kernels: 7.46 us -> 56.9 us
  blocking collectives: 42.4 us -> 0 us
  between operations: 14.5 us -> 1.3 us
  matrix products: 11.2 us -> 0 us
  local copies, waits for them, and re-layouts: 0.03 us -> 6.6 us
  other arithmetic: 7.03 us -> 0.68 us
    reduce_scatter x2 -> x0, waiting for transfers between devices: 90.5 us -> none  [the longest x1 83.9 us: local(): lax.psum_scatter(terms, ('row', 'depth'), scatter_dimension=0, tiled=True)]
    psum x1 -> x0, waiting for transfers between devices: 79.8 us -> none  [local(): lax.psum((weight_part, bias_portion), ('row', 'col', 'depth'))]
    pallas_call x0 -> x1, Pallas kernels: none -> 52.4 us  [run_layer(): pl.pallas_call(functools.partial(layer_kernel, sizes, grad_norm), out_sha...]
    all_gather x1 -> x0, waiting for transfers between devices: 51.7 us -> none  [local(): panel_rows = lax.all_gather(scaled, ('row', 'depth'), axis=0, tiled=True)]
    psum x1 -> x0, blocking collectives: 40.5 us -> none  [local(): lax.psum((weight_part, bias_portion), ('row', 'col', 'depth'))]
    dot_general x5 -> x0, matrix products: 11.2 us -> none  [the longest x1 4.79 us: local(): lax.dot_general(block, group_grad, (((0,), (0,)), ((), ())), preferred_el...]
    unnamed x8 -> x4, local copies, waits for them, and re-layouts: 0.03 us -> 5.84 us
    convert_element_type x3 -> x0, other arithmetic: 4.21 us -> none  [the longest x1 1.63 us: local(): (node_scale * (back_sum + scaled_grad.astype(jnp.float32))).astype(jnp.bf...]
  transfers between devices with their start and end apart: 4 -> 0, of which waited for: 4 -> 0; matrix products, arithmetic and copies ran while one was open for 2% -> 0% of each run, Pallas kernels for 2% -> 0%
where the time goes in v2:
time: 66.4 us; the launch traced here: 65.5 us
  Pallas kernels  56.9 us (86%)
  local copies, waits for them, and re-layouts  6.6 us (10%)
  between operations  1.3 us (2%)
  other arithmetic  0.68 us (1%)
    pallas_call x1, Pallas kernels, run_layer(): pl.pallas_call(functools.partial(layer_kernel, sizes, grad_norm), out_sha...  52.4 us
    unnamed x4, local copies, waits for them, and re-layouts  5.84 us
    pallas_call x1, Pallas kernels, build_block(): pl.pallas_call(functools.partial(build_kernel, chunk), out_shape=jax.Shap...  4.54 us

profile of v2, /device:TPU:0, one launch (start us, length us, event | category | flops | bytes accessed | tf_op | source)
XLA Modules:
  0.0 65.5 jit_solution(4725575568974708599)
XLA Ops:
  1.3 0.7 %convert_rsqrt_fusion = f32[256]{0:T(256)S(1)} fusion(s32[256]{0:T(256)} %param.10), kind=kLoop, calls=%fused_computation | loop fusion | flops 256 | bytes 2048 | tf_op jit(solution)/shard_map/rsqrt | solution.py:366
  2.0 0.8 %broadcast_in_dim.2.scale = f32[256,128]{1,0:T(8,128)} broadcast(f32[256]{0:T(256)S(1)} %convert_rsqrt_fusion), dimensions={0} | broadcast | bytes 132096 | tf_op jit(solution)/shard_map/broadcast_in_dim | solution.py:366
  2.7 4.5 %shard_map.120.block = bf16[512,4096]{1,0:T(8,128)(2,1)} custom-call(s32[256]{0:T(256)} %bitcast.10, s32[256]{0:T(256)} %bitcast.11, s32[1]{0:T(128)} %bitcast.6.count_ref, bf16[256,128,128]{2,1,0:T(8,128)(2,1)} %bitcast.7), custom_call_target="tpu_custom_call" | custom-call | flops 4194304 | bytes 12582912 | tf_op jit(solution)/shard_map/pallas_call | solution.py:54
  7.3 52.4 %shard_map.121 = (bf16[256,256]{1,0:T(8,128)(2,1)}, f32[128,256]{1,0:T(8,128)}, f32[1,256]{1,0:T(1,128)}, bf16[256,128]{1,0:T(8,128)(2,1)}) custom-call(bf16[512,4096]{1,0:T(8,128)(2,1)} %shard_map.120.block, bf16[256,128]{1,0:T(8,128)(2,1)} %features.1, f32[256,128]{1,0:T(8,128)} %broadcast_in_dim.2.scale, bf16[128,256]{1,0:T(8,128)(2,1)} %weight.1, ...), custom_call_target="tpu_custom_call" | custom-call | tf_op jit(solution)/shard_map/pallas_call | solution.py:316
  59.7 1.6 %copy.18 = bf16[256,256]{1,0:T(8,128)(2,1)} copy(bf16[256,256]{1,0:T(8,128)(2,1)} %get-tuple-element.16) | data formatting | bytes 262144
  61.2 1.6 %copy.19 = f32[128,256]{1,0:T(8,128)} copy(f32[128,256]{1,0:T(8,128)} %get-tuple-element.17) | data formatting | bytes 262144
  62.8 1.2 %copy.20 = f32[256]{0:T(256)} copy(f32[256]{0:T(256)} %bitcast.9) | data formatting | bytes 2048
  64.0 1.5 %copy.21 = bf16[256,128]{1,0:T(8,128)(2,1)} copy(bf16[256,128]{1,0:T(8,128)(2,1)} %get-tuple-element.19) | data formatting | bytes 131072

commit v3 on v2

--- a/solution.py
+++ b/solution.py
@@ -75,9 +75,9 @@
 def layer_kernel(
     sizes,
     grad_norm,
-    block,
+    block_hbm,
     features,
-    scale,
+    degree,
     weight,
     bias,
     cotangent,
@@ -85,6 +85,8 @@
     weight_grad,
     bias_grad,
     input_gradient,
+    block,
+    scale,
     panel,
     acc,
     share,
@@ -96,9 +98,11 @@
     deep_recv,
     w_send,
     w_col,
+    w_mid,
     w_row,
     w_deep,
     w_out,
+    block_s,
     panel_s,
     panel_r,
     share_s,
@@ -115,6 +119,8 @@
     wr_r,
     wd_s,
     wd_r,
+    wg_s,
+    wg_r,
     wo_s,
     wo_r,
 ):
@@ -151,6 +157,8 @@
 
     deep_order = sorted(range(1, depths), key=lambda k: (min(k, depths - k), k))
 
+    bring = pltpu.make_async_copy(block_hbm, block, block_s)
+    bring.start()
     barrier = pltpu.get_barrier_semaphore()
     for m in range(1, cols):
         pl.semaphore_signal(barrier, inc=1, device_id={"col": col_of(m)}, device_id_type=pl.DeviceIdType.MESH)
@@ -159,6 +167,8 @@
     for k in range(1, depths):
         pl.semaphore_signal(barrier, inc=1, device_id={"depth": deep_of(k)}, device_id_type=pl.DeviceIdType.MESH)
     mine = me_r * depths + me_d
+    node_scale = lax.rsqrt(degree[...].astype(f32))
+    scale[...] = jnp.broadcast_to(node_scale, features.shape[::-1]).T
     scaled = (features[...].astype(f32) * scale[...]).astype(bf16)
     panel[mine] = scaled
     pl.semaphore_wait(barrier, cols + rows + depths - 3)
@@ -172,6 +182,7 @@
         at = pl.ds(pl.multiple_of(q * nodes, nodes), nodes)
         return jnp.dot(block[:, at], panel[q], preferred_element_type=f32)
 
+    bring.wait()
     acc[...] = product(mine)
     for k in deep_order:
         q = me_r * depths + deep_of(k)
@@ -210,10 +221,12 @@
 
     w_part = lax.dot_general(mixed, pre_grad, (((0,), (0,)), ((), ())), preferred_element_type=f32)
     b_part = jnp.sum(pre_grad.astype(f32).reshape(nodes // 8, 8, pre_grad.shape[1]), axis=0)
-    band = w_part.shape[0] // cols
+    band = w_part.shape[0] // (cols * rows)
     for c in range(cols):
-        w_send[c, :band] = w_part[c * band : (c + 1) * band]
-        w_send[c, band:] = b_part
+        for r in range(rows):
+            first = (c * rows + r) * band
+            w_send[c, r, :8] = b_part
+            w_send[c, r, 8:] = w_part[first : first + band]
     for m in range(1, cols):
         start(w_send.at[col_of(m)], w_col.at[me_c], wc_s.at[m - 1], wc_r.at[m - 1], col=col_of(m))
     w_col[me_c] = w_send[me_c]
@@ -223,7 +236,21 @@
         send(grads.at[c], grads.at[c], grads_s.at[m - 1], grads_r.at[m - 1], col=col_of(m)).wait_recv()
     turned = grads[...].reshape(cols * nodes, scaled_grad.shape[1]).T
 
-    for k in deep_order + [0]:
+    def total(buffer, count):
+        value = buffer[0]
+        for i in range(1, count):
+            value = value + buffer[i]
+        return value
+
+    for m in range(1, cols):
+        c = lax.rem(me_c + cols - m, cols)
+        send(w_send.at[c], w_col.at[c], wc_s.at[m - 1], wc_r.at[m - 1], col=col_of(m)).wait_recv()
+    w_mid[...] = total(w_col, cols)
+    for j in range(1, rows):
+        start(w_mid.at[row_of(j)], w_row.at[me_r], wr_s.at[j - 1], wr_r.at[j - 1], row=row_of(j))
+    w_row[me_r] = w_mid[me_r]
+
+    def back_terms(k):
         for j in list(range(1, rows)) + [0]:
             q = row_of(j) * depths + deep_of(k)
             at = pl.ds(pl.multiple_of(q * nodes, nodes), nodes)
@@ -240,17 +267,25 @@
                     row=row_of(j),
                 )
 
-    def total(buffer, count):
-        value = buffer[0]
-        for i in range(1, count):
-            value = value + buffer[i]
-        return value
-
-    for m in range(1, cols):
-        send(w_send.at[me_c], w_col.at[me_c], wc_s.at[m - 1], wc_r.at[m - 1], col=col_of(m)).wait_recv()
-    w_row[me_r] = total(w_col, cols)
-    for j in range(1, rows):
-        start(w_row.at[me_r], w_row.at[me_r], wr_s.at[j - 1], wr_r.at[j - 1], row=row_of(j))
+    back_order = deep_order + [0]
+    back_terms(back_order[0])
+    for j in range(1, rows):
+        r = row_of(rows - j)
+        send(w_mid.at[r], w_row.at[r], wr_s.at[j - 1], wr_r.at[j - 1], row=row_of(j)).wait_recv()
+    w_deep[me_d] = total(w_row, rows)
+    for k in range(1, depths):
+        start(w_deep.at[me_d], w_deep.at[me_d], wd_s.at[k - 1], wd_r.at[k - 1], depth=deep_of(k))
+    for k in back_order[1:]:
+        back_terms(k)
+    for k in range(1, depths):
+        send(
+            w_deep.at[me_d], w_deep.at[deep_of(depths - k)], wd_s.at[k - 1], wd_r.at[k - 1], depth=deep_of(k)
+        ).wait_recv()
+    w_total = total(w_deep, depths) * grad_norm
+    w_out[me_c, me_r] = w_total[8:]
+    bias_grad[...] = jnp.sum(w_total[:8], axis=0, keepdims=True)
+    for j in range(1, rows):
+        start(w_out.at[me_c, me_r], w_out.at[me_c, me_r], wg_s.at[j - 1], wg_r.at[j - 1], row=row_of(j))
 
     def row_sum(k):
         value = back_own[k]
@@ -269,21 +304,11 @@
         deep_send[k - 1] = row_sum(k).astype(bf16)
         start(deep_send.at[k - 1], deep_recv.at[k - 1], deep_s.at[k - 1], deep_r.at[k - 1], depth=deep_of(k))
 
-    for j in range(1, rows):
-        send(w_row.at[me_r], w_row.at[row_of(rows - j)], wr_s.at[j - 1], wr_r.at[j - 1], row=row_of(j)).wait_recv()
-    w_deep[me_d] = total(w_row, rows)
-    for k in range(1, depths):
-        start(w_deep.at[me_d], w_deep.at[me_d], wd_s.at[k - 1], wd_r.at[k - 1], depth=deep_of(k))
-
     back = row_sum(0)
 
-    for k in range(1, depths):
-        send(
-            w_deep.at[me_d], w_deep.at[deep_of(depths - k)], wd_s.at[k - 1], wd_r.at[k - 1], depth=deep_of(k)
-        ).wait_recv()
-    w_total = total(w_deep, depths) * grad_norm
-    w_out[me_c] = w_total[:band]
-    bias_grad[...] = jnp.sum(w_total[band:], axis=0, keepdims=True)
+    for j in range(1, rows):
+        r = row_of(rows - j)
+        send(w_out.at[me_c, r], w_out.at[me_c, r], wg_s.at[j - 1], wg_r.at[j - 1], row=row_of(j)).wait_recv()
     for m in range(1, cols):
         start(w_out.at[me_c], w_out.at[me_c], wo_s.at[m - 1], wo_r.at[m - 1], col=col_of(m))
 
@@ -298,16 +323,39 @@
         c = lax.rem(me_c + cols - m, cols)
         send(w_out.at[c], w_out.at[c], wo_s.at[m - 1], wo_r.at[m - 1], col=col_of(m)).wait_recv()
     for c in range(cols):
-        weight_grad[c * band : (c + 1) * band] = w_out[c]
+        for r in range(rows):
+            first = (c * rows + r) * band
+            weight_grad[first : first + band] = w_out[c, r]
     for copy in sent:
         copy.wait_send()
 
 
-def run_layer(sizes, grad_norm, block, features, scale, weight, bias, cotangent):
+def finish_kernel(*refs):
+    count = (len(refs) - 1) // 2
+    sems = refs[-1]
+    copies = [pltpu.make_async_copy(refs[i], refs[count + i], sems.at[i]) for i in range(count)]
+    for copy in copies:
+        copy.start()
+    for copy in copies:
+        copy.wait()
+
+
+def finish(*arrays):
+    anywhere = pl.BlockSpec(memory_space=pl.ANY)
+    return pl.pallas_call(
+        finish_kernel,
+        out_shape=tuple(jax.ShapeDtypeStruct(a.shape, a.dtype) for a in arrays),
+        in_specs=[anywhere] * len(arrays),
+        out_specs=(anywhere,) * len(arrays),
+        scratch_shapes=[pltpu.SemaphoreType.DMA((len(arrays),))],
+    )(*arrays)
+
+
+def run_layer(sizes, grad_norm, block, features, degree, weight, bias, cotangent):
     rows, cols, depths = sizes
     nodes, width = features.shape
     wide = weight.shape[1]
-    band = width // cols
+    band = width // (cols * rows)
     f32, bf16 = jnp.float32, jnp.bfloat16
 
     def dma(*shape):
@@ -321,9 +369,11 @@
             jax.ShapeDtypeStruct((1, wide), f32),
             jax.ShapeDtypeStruct((nodes, width), bf16),
         ),
-        in_specs=[pl.BlockSpec(memory_space=pltpu.VMEM)] * 6,
+        in_specs=[pl.BlockSpec(memory_space=pl.ANY)] + [pl.BlockSpec(memory_space=pltpu.VMEM)] * 5,
         out_specs=(pl.BlockSpec(memory_space=pltpu.VMEM),) * 4,
         scratch_shapes=[
+            pltpu.VMEM(block.shape, bf16),
+            pltpu.VMEM((nodes, width), f32),
             pltpu.VMEM((rows * depths, nodes, width), bf16),
             pltpu.VMEM((cols * nodes, width), f32),
             pltpu.VMEM((cols - 1, nodes, width), f32),
@@ -333,11 +383,13 @@
             pltpu.VMEM((depths, rows - 1, width, nodes), bf16),
             pltpu.VMEM((depths - 1, width, nodes), bf16),
             pltpu.VMEM((depths - 1, width, nodes), bf16),
-            pltpu.VMEM((cols, band + 8, wide), f32),
-            pltpu.VMEM((cols, band + 8, wide), f32),
+            pltpu.VMEM((cols, rows, band + 8, wide), f32),
+            pltpu.VMEM((cols, rows, band + 8, wide), f32),
+            pltpu.VMEM((rows, band + 8, wide), f32),
             pltpu.VMEM((rows, band + 8, wide), f32),
             pltpu.VMEM((depths, band + 8, wide), f32),
-            pltpu.VMEM((cols, band, wide), f32),
+            pltpu.VMEM((cols, rows, band, wide), f32),
+            pltpu.SemaphoreType.DMA(()),
             pltpu.SemaphoreType.DMA((depths, rows)),
             pltpu.SemaphoreType.DMA((rows * depths,)),
             *dma(cols - 1),
@@ -347,12 +399,13 @@
             *dma(cols - 1),
             *dma(rows - 1),
             *dma(depths - 1),
+            *dma(rows - 1),
             *dma(cols - 1),
         ],
         compiler_params=pltpu.CompilerParams(
             collective_id=0, has_side_effects=True, vmem_limit_bytes=56 * 1024 * 1024
         ),
-    )(block, features, scale, weight, bias, cotangent)
+    )(block, features, degree, weight, bias, cotangent)
 
 
 def local(features, degree, tiles, tile_rows, tile_cols, tile_count, weight, bias, cotangent):
@@ -363,7 +416,6 @@
     row_tiles = sizes[1] * node_dev // tile_size
     span = sizes[0] * sizes[2] * node_dev // tile_size
     grad_norm = (node_dev * sizes[0] * sizes[1] * sizes[2]) ** (-0.5)
-    scale = jnp.broadcast_to(lax.rsqrt(degree.astype(jnp.float32))[:, None], features.shape)
     block = build_block(
         tiles.reshape(slot_total, tile_size, tile_size),
         tile_rows.reshape(slot_total),
@@ -372,9 +424,10 @@
         row_tiles,
         span,
     )
-    hidden, weight_grad, bias_grad, input_gradient = run_layer(
-        sizes, grad_norm, block, features, scale, weight, bias.reshape(1, -1), cotangent
+    results = run_layer(
+        sizes, grad_norm, block, features, degree.reshape(1, -1), weight, bias.reshape(1, -1), cotangent
     )
+    hidden, weight_grad, bias_grad, input_gradient = finish(*results)
     return (hidden, weight_grad, bias_grad.reshape(-1), input_gradient)
 
 

time: 66.4 us -> 62.3 us (0.938)
  local copies, waits for them, and re-layouts: 6.6 us -> 0 us
  Pallas kernels: 56.9 us -> 60.4 us
  other arithmetic: 0.68 us -> 0 us
    pallas_call x0 -> x1, Pallas kernels: none -> 11.1 us  [finish(): pl.pallas_call(finish_kernel, out_shape=tuple((jax.ShapeDtypeStruct(a.sha...]
    pallas_call x1, Pallas kernels: 52.4 us -> 44.1 us  [run_layer(): pl.pallas_call(functools.partial(layer_kernel, sizes, grad_norm), out_sha...]
    unnamed x4 -> x0, local copies, waits for them, and re-layouts: 5.84 us -> none
    broadcast_in_dim x1 -> x0, local copies, waits for them, and re-layouts: 0.76 us -> none  [local(): jnp.broadcast_to(lax.rsqrt(degree.astype(jnp.float32))[:, None], features...]
    pallas_call x1, Pallas kernels: 4.54 us -> 5.26 us  [build_block(): pl.pallas_call(functools.partial(build_kernel, chunk), out_shape=jax.Shap...]
    rsqrt x1 -> x0, other arithmetic: 0.68 us -> none  [local(): lax.rsqrt(degree.astype(jnp.float32))[:, None]]
where the time goes in v3:
time: 62.3 us; the launch traced here: 61.7 us
  Pallas kernels  60.4 us (97%)
  between operations  1.29 us (2%)
    pallas_call x1, Pallas kernels, run_layer(): pl.pallas_call(functools.partial(layer_kernel, sizes, grad_norm), out_sha...  44.1 us
    pallas_call x1, Pallas kernels, finish(): pl.pallas_call(finish_kernel, out_shape=tuple((jax.ShapeDtypeStruct(a.sha...  11.1 us
    pallas_call x1, Pallas kernels, build_block(): pl.pallas_call(functools.partial(build_kernel, chunk), out_shape=jax.Shap...  5.26 us

profile of v3, /device:TPU:0, one launch (start us, length us, event | category | flops | bytes accessed | tf_op | source)
XLA Modules:
  0.0 61.7 jit_solution(1971069668457632772)
XLA Ops:
  1.3 5.3 %shard_map.120.block_hbm = bf16[512,4096]{1,0:T(8,128)(2,1)} custom-call(s32[256]{0:T(256)} %bitcast.11, s32[256]{0:T(256)} %bitcast.12, s32[1]{0:T(128)} %bitcast.7.count_ref, bf16[256,128,128]{2,1,0:T(8,128)(2,1)} %bitcast.8), custom_call_target="tpu_custom_call" | custom-call | flops 4194304 | bytes 12582912 | tf_op jit(solution)/shard_map/pallas_call | solution.py:54
  6.5 44.1 %shard_map.121 = (bf16[256,256]{1,0:T(8,128)(2,1)}, f32[128,256]{1,0:T(8,128)}, f32[1,256]{1,0:T(1,128)}, bf16[256,128]{1,0:T(8,128)(2,1)}) custom-call(bf16[512,4096]{1,0:T(8,128)(2,1)} %shard_map.120.block_hbm, bf16[256,128]{1,0:T(8,128)(2,1)} %features.1, s32[1,256]{1,0:T(1,128)} %bitcast.9, bf16[128,256]{1,0:T(8,128)(2,1)} %weight.1, f32[1,256]{1,0:T(1,128)} %bitcast.10, ...), custom_call_target="tpu_custom_call" | custom-call | tf_op jit(solution)/shard_map/pallas_call | solution.py:364
  50.6 11.1 %shard_map.122 = (bf16[256,256]{1,0:T(8,128)(2,1)}, f32[128,256]{1,0:T(8,128)}, f32[1,256]{1,0:T(1,128)}, bf16[256,128]{1,0:T(8,128)(2,1)}) custom-call(bf16[256,256]{1,0:T(8,128)(2,1)} %get-tuple-element.12.refs_0_, f32[128,256]{1,0:T(8,128)} %get-tuple-element.13.refs_1_, f32[1,256]{1,0:T(1,128)} %get-tuple-element.14.refs_2_, ...), custom_call_target="tpu_custom_call" | custom-call | tf_op jit(solution)/shard_map/pallas_call | solution.py:345

commit v4 on v3

--- a/solution.py
+++ b/solution.py
@@ -331,23 +331,18 @@
 
 
 def finish_kernel(*refs):
-    count = (len(refs) - 1) // 2
-    sems = refs[-1]
-    copies = [pltpu.make_async_copy(refs[i], refs[count + i], sems.at[i]) for i in range(count)]
-    for copy in copies:
-        copy.start()
-    for copy in copies:
-        copy.wait()
+    count = len(refs) // 2
+    for i in range(count):
+        refs[count + i][...] = refs[i][...]
 
 
 def finish(*arrays):
-    anywhere = pl.BlockSpec(memory_space=pl.ANY)
+    vmem = pl.BlockSpec(memory_space=pltpu.VMEM)
     return pl.pallas_call(
         finish_kernel,
         out_shape=tuple(jax.ShapeDtypeStruct(a.shape, a.dtype) for a in arrays),
-        in_specs=[anywhere] * len(arrays),
-        out_specs=(anywhere,) * len(arrays),
-        scratch_shapes=[pltpu.SemaphoreType.DMA((len(arrays),))],
+        in_specs=[vmem] * len(arrays),
+        out_specs=(vmem,) * len(arrays),
     )(*arrays)
 
 

time: 62.3 us -> 52.9 us (0.85)
  Pallas kernels: 60.4 us -> 50.9 us
    pallas_call x1, Pallas kernels: 11.1 us -> 1.7 us  [finish(): pl.pallas_call(finish_kernel, out_shape=tuple((jax.ShapeDtypeStruct(a.sha...]
    pallas_call x1, Pallas kernels: 44.1 us -> 42.7 us  [run_layer(): pl.pallas_call(functools.partial(layer_kernel, sizes, grad_norm), out_sha...]
    pallas_call x1, Pallas kernels: 5.26 us -> 6.48 us  [build_block(): pl.pallas_call(functools.partial(build_kernel, chunk), out_shape=jax.Shap...]
where the time goes in v4:
time: 52.9 us; the launch traced here: 52.2 us
  Pallas kernels  50.9 us (96%)
  between operations  1.29 us (2%)
    pallas_call x1, Pallas kernels, run_layer(): pl.pallas_call(functools.partial(layer_kernel, sizes, grad_norm), out_sha...  42.7 us
    pallas_call x1, Pallas kernels, build_block(): pl.pallas_call(functools.partial(build_kernel, chunk), out_shape=jax.Shap...  6.48 us
    pallas_call x1, Pallas kernels, finish(): pl.pallas_call(finish_kernel, out_shape=tuple((jax.ShapeDtypeStruct(a.sha...  1.7 us

profile of v4, /device:TPU:0, one launch (start us, length us, event | category | flops | bytes accessed | tf_op | source)
XLA Modules:
  0.0 52.2 jit_solution(3736029641026923174)
XLA Ops:
  1.3 6.5 %shard_map.120.block_hbm = bf16[512,4096]{1,0:T(8,128)(2,1)} custom-call(s32[256]{0:T(256)} %bitcast.11, s32[256]{0:T(256)} %bitcast.12, s32[1]{0:T(128)} %bitcast.7.count_ref, bf16[256,128,128]{2,1,0:T(8,128)(2,1)} %bitcast.8), custom_call_target="tpu_custom_call" | custom-call | flops 4194304 | bytes 12582912 | tf_op jit(solution)/shard_map/pallas_call | solution.py:54
  7.8 42.7 %shard_map.121 = (bf16[256,256]{1,0:T(8,128)(2,1)}, f32[128,256]{1,0:T(8,128)}, f32[1,256]{1,0:T(1,128)}, bf16[256,128]{1,0:T(8,128)(2,1)}) custom-call(bf16[512,4096]{1,0:T(8,128)(2,1)} %shard_map.120.block_hbm, bf16[256,128]{1,0:T(8,128)(2,1)} %features.1, s32[1,256]{1,0:T(1,128)} %bitcast.9, bf16[128,256]{1,0:T(8,128)(2,1)} %weight.1, f32[1,256]{1,0:T(1,128)} %bitcast.10, ...), custom_call_target="tpu_custom_call" | custom-call | tf_op jit(solution)/shard_map/pallas_call | solution.py:359
  50.5 1.7 %shard_map.122 = (bf16[256,256]{1,0:T(8,128)(2,1)}, f32[128,256]{1,0:T(8,128)}, f32[1,256]{1,0:T(1,128)}, bf16[256,128]{1,0:T(8,128)(2,1)}) custom-call(bf16[256,256]{1,0:T(8,128)(2,1)} %get-tuple-element.12.refs_0_, f32[128,256]{1,0:T(8,128)} %get-tuple-element.13.refs_1_, f32[1,256]{1,0:T(1,128)} %get-tuple-element.14.refs_2_, ...), custom_call_target="tpu_custom_call" | custom-call | tf_op jit(solution)/shard_map/pallas_call | solution.py:341

commit v5 on v4

--- a/solution.py
+++ b/solution.py
@@ -92,6 +92,7 @@
     share,
     grads,
     back_own,
+    back_held,
     back_send,
     back_row,
     deep_send,
@@ -105,12 +106,16 @@
     block_s,
     panel_s,
     panel_r,
+    panel_f,
+    panel_h,
     share_s,
     share_r,
     grads_s,
     grads_r,
     back_s,
     back_r,
+    relay_s,
+    relay_r,
     deep_s,
     deep_r,
     wc_s,
@@ -129,6 +134,8 @@
     me_r, me_c, me_d = (lax.axis_index(name) for name in ("row", "col", "depth"))
     f32, bf16 = jnp.float32, jnp.bfloat16
 
+    corner = (me_r, me_r + 1 - 2 * lax.rem(me_r, 2), lax.rem(me_r + 2, 4), 3 - me_r)
+
     def row_of(j):
         return lax.rem(me_r + j, rows)
 
@@ -175,8 +182,8 @@
 
     for k in deep_order:
         start(panel.at[mine], panel.at[mine], panel_s.at[k, 0], panel_r.at[mine], depth=deep_of(k))
-    for j in range(1, rows):
-        start(panel.at[mine], panel.at[mine], panel_s.at[0, j], panel_r.at[mine], row=row_of(j))
+    for j in (1, 2):
+        start(panel.at[mine], panel.at[mine], panel_s.at[0, j], panel_r.at[mine], row=corner[j])
 
     def product(q):
         at = pl.ds(pl.multiple_of(q * nodes, nodes), nodes)
@@ -184,17 +191,33 @@
 
     bring.wait()
     acc[...] = product(mine)
-    for k in deep_order:
+    half = nodes // 2
+
+    def part(q, h):
+        return panel.at[q, pl.ds(h * half, half)]
+
+    def from_neighbours(k):
+        for j in (1, 2):
+            q = corner[j] * depths + deep_of(k)
+            send(panel.at[q], panel.at[q], panel_s.at[k, j], panel_r.at[q], row=corner[j]).wait_recv()
+            arrived = panel_r if j == 1 else panel_h
+            start(part(q, j - 1), part(q, j - 1), panel_f.at[k, j - 1], arrived.at[q], row=corner[3 - j])
+            acc[...] += product(q)
+
+    order = [0] + deep_order
+    for i, k in enumerate(deep_order):
         q = me_r * depths + deep_of(k)
         send(panel.at[q], panel.at[q], panel_s.at[k, 0], panel_r.at[q], depth=deep_of(k)).wait_recv()
-        for j in range(1, rows):
-            start(panel.at[q], panel.at[q], panel_s.at[k, j], panel_r.at[q], row=row_of(j))
+        for j in (1, 2):
+            start(panel.at[q], panel.at[q], panel_s.at[k, j], panel_r.at[q], row=corner[j])
         acc[...] += product(q)
-    for k in [0] + deep_order:
-        for j in range(1, rows):
-            q = row_of(j) * depths + deep_of(k)
-            send(panel.at[q], panel.at[q], panel_s.at[k, j], panel_r.at[q], row=row_of(j)).wait_recv()
-            acc[...] += product(q)
+        from_neighbours(order[i])
+    from_neighbours(order[-1])
+    for k in order:
+        q = corner[3] * depths + deep_of(k)
+        send(part(q, 0), part(q, 0), panel_f.at[k, 0], panel_r.at[q], row=corner[2]).wait_recv()
+        send(part(q, 1), part(q, 1), panel_f.at[k, 1], panel_h.at[q], row=corner[1]).wait_recv()
+        acc[...] += product(q)
 
     def acc_of(c):
         return acc.at[pl.ds(pl.multiple_of(c * nodes, nodes), nodes)]
@@ -250,33 +273,60 @@
         start(w_mid.at[row_of(j)], w_row.at[me_r], wr_s.at[j - 1], wr_r.at[j - 1], row=row_of(j))
     w_row[me_r] = w_mid[me_r]
 
+    edge = features.shape[1] // 2
+
+    def relay(k, h, peer):
+        at = pl.ds(h * edge, edge)
+        sems = (back_s.at[k, 2], back_r.at[k, 2]) if h == 0 else (relay_s.at[k], relay_r.at[k])
+        return (back_send.at[k, 2, at], back_row.at[k, 2, at], *sems), {"row": corner[peer]}
+
     def back_terms(k):
-        for j in list(range(1, rows)) + [0]:
-            q = row_of(j) * depths + deep_of(k)
+        for j in (3, 1, 2, 0):
+            q = corner[j] * depths + deep_of(k)
             at = pl.ds(pl.multiple_of(q * nodes, nodes), nodes)
             term = jnp.dot(turned, block[:, at], preferred_element_type=f32)
             if j == 0:
                 back_own[k] = term
+            elif j == 3:
+                back_send[k, 2] = term.astype(bf16)
+                for h in (0, 1):
+                    args, peer = relay(k, h, h + 1)
+                    start(*args, **peer)
             else:
-                back_send[k, j - 1] = term.astype(bf16)
-                start(
-                    back_send.at[k, j - 1],
-                    back_row.at[k, j - 1],
-                    back_s.at[k, j - 1],
-                    back_r.at[k, j - 1],
-                    row=row_of(j),
-                )
+                back_held[k, j - 1] = term
+
+    def back_pass(k):
+        for h in (0, 1):
+            args, peer = relay(k, h, h + 1)
+            send(*args, **peer).wait_recv()
+        low, high = pl.ds(0, edge), pl.ds(edge, edge)
+        back_send[k, 0, low] = back_held[k, 0, low].astype(bf16)
+        back_send[k, 0, high] = (back_held[k, 0, high] + back_row[k, 2, high].astype(f32)).astype(bf16)
+        back_send[k, 1, low] = (back_held[k, 1, low] + back_row[k, 2, low].astype(f32)).astype(bf16)
+        back_send[k, 1, high] = back_held[k, 1, high].astype(bf16)
+        for j in (1, 2):
+            start(
+                back_send.at[k, j - 1],
+                back_row.at[k, j - 1],
+                back_s.at[k, j - 1],
+                back_r.at[k, j - 1],
+                row=corner[j],
+            )
 
     back_order = deep_order + [0]
     back_terms(back_order[0])
+    back_terms(back_order[1])
+    back_pass(back_order[0])
     for j in range(1, rows):
         r = row_of(rows - j)
         send(w_mid.at[r], w_row.at[r], wr_s.at[j - 1], wr_r.at[j - 1], row=row_of(j)).wait_recv()
     w_deep[me_d] = total(w_row, rows)
     for k in range(1, depths):
         start(w_deep.at[me_d], w_deep.at[me_d], wd_s.at[k - 1], wd_r.at[k - 1], depth=deep_of(k))
-    for k in back_order[1:]:
-        back_terms(k)
+    for i in range(1, depths):
+        if i + 1 < depths:
+            back_terms(back_order[i + 1])
+        back_pass(back_order[i])
     for k in range(1, depths):
         send(
             w_deep.at[me_d], w_deep.at[deep_of(depths - k)], wd_s.at[k - 1], wd_r.at[k - 1], depth=deep_of(k)
@@ -289,13 +339,13 @@
 
     def row_sum(k):
         value = back_own[k]
-        for j in range(1, rows):
+        for j in (1, 2):
             send(
                 back_send.at[k, j - 1],
                 back_row.at[k, j - 1],
                 back_s.at[k, j - 1],
                 back_r.at[k, j - 1],
-                row=row_of(j),
+                row=corner[j],
             ).wait_recv()
             value = value + back_row[k, j - 1].astype(f32)
         return value
@@ -374,6 +424,7 @@
             pltpu.VMEM((cols - 1, nodes, width), f32),
             pltpu.VMEM((cols, nodes, width), bf16),
             pltpu.VMEM((depths, width, nodes), f32),
+            pltpu.VMEM((depths, 2, width, nodes), f32),
             pltpu.VMEM((depths, rows - 1, width, nodes), bf16),
             pltpu.VMEM((depths, rows - 1, width, nodes), bf16),
             pltpu.VMEM((depths - 1, width, nodes), bf16),
@@ -387,9 +438,12 @@
             pltpu.SemaphoreType.DMA(()),
             pltpu.SemaphoreType.DMA((depths, rows)),
             pltpu.SemaphoreType.DMA((rows * depths,)),
+            pltpu.SemaphoreType.DMA((depths, 2)),
+            pltpu.SemaphoreType.DMA((rows * depths,)),
             *dma(cols - 1),
             *dma(cols - 1),
             *dma(depths, rows - 1),
+            *dma(depths),
             *dma(depths - 1),
             *dma(cols - 1),
             *dma(rows - 1),

time: 52.9 us -> 53.5 us (1.011); the launches traced: 52.2 us -> 53.8 us
  Pallas kernels: 50.9 us -> 52.5 us
    pallas_call x1, Pallas kernels: 42.7 us -> 44.2 us  [run_layer(): pl.pallas_call(functools.partial(layer_kernel, sizes, grad_norm), out_sha...]
where the time goes in v5:
time: 53.5 us; the launch traced here: 53.8 us
  Pallas kernels  52.5 us (98%)
  between operations  1.29 us (2%)
    pallas_call x1, Pallas kernels, run_layer(): pl.pallas_call(functools.partial(layer_kernel, sizes, grad_norm), out_sha...  44.2 us
    pallas_call x1, Pallas kernels, build_block(): pl.pallas_call(functools.partial(build_kernel, chunk), out_shape=jax.Shap...  6.56 us
    pallas_call x1, Pallas kernels, finish(): pl.pallas_call(finish_kernel, out_shape=tuple((jax.ShapeDtypeStruct(a.sha...  1.7 us

profile of v5, /device:TPU:0, one launch (start us, length us, event | category | flops | bytes accessed | tf_op | source)
XLA Modules:
  0.0 53.8 jit_solution(16574880135223566107)
XLA Ops:
  1.3 6.6 %shard_map.120.block_hbm = bf16[512,4096]{1,0:T(8,128)(2,1)} custom-call(s32[256]{0:T(256)} %bitcast.11, s32[256]{0:T(256)} %bitcast.12, s32[1]{0:T(128)} %bitcast.7.count_ref, bf16[256,128,128]{2,1,0:T(8,128)(2,1)} %bitcast.8), custom_call_target="tpu_custom_call" | custom-call | flops 4194304 | bytes 12582912 | tf_op jit(solution)/shard_map/pallas_call | solution.py:54
  7.8 44.2 %shard_map.121 = (bf16[256,256]{1,0:T(8,128)(2,1)}, f32[128,256]{1,0:T(8,128)}, f32[1,256]{1,0:T(1,128)}, bf16[256,128]{1,0:T(8,128)(2,1)}) custom-call(bf16[512,4096]{1,0:T(8,128)(2,1)} %shard_map.120.block_hbm, bf16[256,128]{1,0:T(8,128)(2,1)} %features.1, s32[1,256]{1,0:T(1,128)} %bitcast.9, bf16[128,256]{1,0:T(8,128)(2,1)} %weight.1, f32[1,256]{1,0:T(1,128)} %bitcast.10, ...), custom_call_target="tpu_custom_call" | custom-call | tf_op jit(solution)/shard_map/pallas_call | solution.py:409
  52.1 1.7 %shard_map.122 = (bf16[256,256]{1,0:T(8,128)(2,1)}, f32[128,256]{1,0:T(8,128)}, f32[1,256]{1,0:T(1,128)}, bf16[256,128]{1,0:T(8,128)(2,1)}) custom-call(bf16[256,256]{1,0:T(8,128)(2,1)} %get-tuple-element.12.refs_0_, f32[128,256]{1,0:T(8,128)} %get-tuple-element.13.refs_1_, f32[1,256]{1,0:T(1,128)} %get-tuple-element.14.refs_2_, ...), custom_call_target="tpu_custom_call" | custom-call | tf_op jit(solution)/shard_map/pallas_call | solution.py:391

commit v6 on v4

--- a/solution.py
+++ b/solution.py
@@ -43,7 +43,14 @@
         @pl.when(k * chunk < live)
         def _():
             fetch(k).wait()
-            lax.fori_loop(k * chunk, jnp.minimum((k + 1) * chunk, live), add, 0)
+
+        @pl.when((k + 1) * chunk <= live)
+        def _():
+            lax.fori_loop(k * chunk, (k + 1) * chunk, add, 0, unroll=8)
+
+        @pl.when(((k + 1) * chunk > live) & (k * chunk < live))
+        def _():
+            lax.fori_loop(k * chunk, live, add, 0)
 
 
 def build_block(tiles, rows, cols, count, row_tiles, col_tiles):

time: 52.9 us -> 51.3 us (0.970); the launches traced: 52.2 us -> 51.2 us
  Pallas kernels: 50.9 us -> 49.9 us
    pallas_call x1, Pallas kernels: 42.7 us -> 41.8 us  [run_layer(): pl.pallas_call(functools.partial(layer_kernel, sizes, grad_norm), out_sha...]
where the time goes in v6:
time: 51.3 us; the launch traced here: 51.2 us
  Pallas kernels  49.9 us (97%)
  between operations  1.29 us (3%)
    pallas_call x1, Pallas kernels, run_layer(): pl.pallas_call(functools.partial(layer_kernel, sizes, grad_norm), out_sha...  41.8 us
    pallas_call x1, Pallas kernels, build_block(): pl.pallas_call(functools.partial(build_kernel, chunk), out_shape=jax.Shap...  6.4 us
    pallas_call x1, Pallas kernels, finish(): pl.pallas_call(finish_kernel, out_shape=tuple((jax.ShapeDtypeStruct(a.sha...  1.7 us

profile of v6, /device:TPU:0, one launch (start us, length us, event | category | flops | bytes accessed | tf_op | source)
XLA Modules:
  0.0 51.2 jit_solution(14848055950089734280)
XLA Ops:
  1.3 6.4 %shard_map.120.block_hbm = bf16[512,4096]{1,0:T(8,128)(2,1)} custom-call(s32[256]{0:T(256)} %bitcast.11, s32[256]{0:T(256)} %bitcast.12, s32[1]{0:T(128)} %bitcast.7.count_ref, bf16[256,128,128]{2,1,0:T(8,128)(2,1)} %bitcast.8), custom_call_target="tpu_custom_call" | custom-call | flops 4194304 | bytes 12582912 | tf_op jit(solution)/shard_map/pallas_call | solution.py:61
  7.7 41.8 %shard_map.121 = (bf16[256,256]{1,0:T(8,128)(2,1)}, f32[128,256]{1,0:T(8,128)}, f32[1,256]{1,0:T(1,128)}, bf16[256,128]{1,0:T(8,128)(2,1)}) custom-call(bf16[512,4096]{1,0:T(8,128)(2,1)} %shard_map.120.block_hbm, bf16[256,128]{1,0:T(8,128)(2,1)} %features.1, s32[1,256]{1,0:T(1,128)} %bitcast.9, bf16[128,256]{1,0:T(8,128)(2,1)} %weight.1, f32[1,256]{1,0:T(1,128)} %bitcast.10, ...), custom_call_target="tpu_custom_call" | custom-call | tf_op jit(solution)/shard_map/pallas_call | solution.py:366
  49.5 1.7 %shard_map.122 = (bf16[256,256]{1,0:T(8,128)(2,1)}, f32[128,256]{1,0:T(8,128)}, f32[1,256]{1,0:T(1,128)}, bf16[256,128]{1,0:T(8,128)(2,1)}) custom-call(bf16[256,256]{1,0:T(8,128)(2,1)} %get-tuple-element.12.refs_0_, f32[128,256]{1,0:T(8,128)} %get-tuple-element.13.refs_1_, f32[1,256]{1,0:T(1,128)} %get-tuple-element.14.refs_2_, ...), custom_call_target="tpu_custom_call" | custom-call | tf_op jit(solution)/shard_map/pallas_call | solution.py:348

commit v7 on v6

--- a/solution.py
+++ b/solution.py
@@ -30,12 +30,23 @@
 
     lax.fori_loop(0, out_ref.shape[0] // 16, clear, 0)
 
-    def add(t, carry):
-        at = (
+    def place(t):
+        return (
             pl.ds(pl.multiple_of(rows_ref[t] * tile, tile), tile),
             pl.ds(pl.multiple_of(cols_ref[t] * tile, tile), tile),
         )
-        out_ref[at] = out_ref[at] + held[t]
+
+    def add(t, carry):
+        out_ref[place(t)] = out_ref[place(t)] + held[t]
+        return carry
+
+    def add_pair(i, carry):
+        t, u = 2 * i, 2 * i + 1
+        same = (rows_ref[t] == rows_ref[u]) & (cols_ref[t] == cols_ref[u])
+        one, two = out_ref[place(t)], out_ref[place(u)]
+        one = one + held[t]
+        out_ref[place(t)] = one
+        out_ref[place(u)] = jnp.where(same, one, two) + held[u]
         return carry
 
     for k in range(slots // chunk):
@@ -46,7 +57,7 @@
 
         @pl.when((k + 1) * chunk <= live)
         def _():
-            lax.fori_loop(k * chunk, (k + 1) * chunk, add, 0, unroll=8)
+            lax.fori_loop(k * chunk // 2, (k + 1) * chunk // 2, add_pair, 0, unroll=4)
 
         @pl.when(((k + 1) * chunk > live) & (k * chunk < live))
         def _():

time: 51.3 us -> 51.9 us (1.012)
    pallas_call x1, Pallas kernels: 41.8 us -> 43 us  [run_layer(): pl.pallas_call(functools.partial(layer_kernel, sizes, grad_norm), out_sha...]
    pallas_call x1, Pallas kernels: 6.4 us -> 5.71 us  [build_block(): pl.pallas_call(functools.partial(build_kernel, chunk), out_shape=jax.Shap...]
where the time goes in v7:
time: 51.9 us; the launch traced here: 51.7 us
  Pallas kernels  50.4 us (97%)
  between operations  1.29 us (2%)
    pallas_call x1, Pallas kernels, run_layer(): pl.pallas_call(functools.partial(layer_kernel, sizes, grad_norm), out_sha...  43 us
    pallas_call x1, Pallas kernels, build_block(): pl.pallas_call(functools.partial(build_kernel, chunk), out_shape=jax.Shap...  5.71 us
    pallas_call x1, Pallas kernels, finish(): pl.pallas_call(finish_kernel, out_shape=tuple((jax.ShapeDtypeStruct(a.sha...  1.7 us

profile of v7, /device:TPU:0, one launch (start us, length us, event | category | flops | bytes accessed | tf_op | source)
XLA Modules:
  0.0 51.7 jit_solution(17257356297524046023)
XLA Ops:
  1.3 5.7 %shard_map.120.block_hbm = bf16[512,4096]{1,0:T(8,128)(2,1)} custom-call(s32[256]{0:T(256)} %bitcast.11, s32[256]{0:T(256)} %bitcast.12, s32[1]{0:T(128)} %bitcast.7.count_ref, bf16[256,128,128]{2,1,0:T(8,128)(2,1)} %bitcast.8), custom_call_target="tpu_custom_call" | custom-call | flops 4194304 | bytes 12582912 | tf_op jit(solution)/shard_map/pallas_call | solution.py:72
  7.0 43.0 %shard_map.121 = (bf16[256,256]{1,0:T(8,128)(2,1)}, f32[128,256]{1,0:T(8,128)}, f32[1,256]{1,0:T(1,128)}, bf16[256,128]{1,0:T(8,128)(2,1)}) custom-call(bf16[512,4096]{1,0:T(8,128)(2,1)} %shard_map.120.block_hbm, bf16[256,128]{1,0:T(8,128)(2,1)} %features.1, s32[1,256]{1,0:T(1,128)} %bitcast.9, bf16[128,256]{1,0:T(8,128)(2,1)} %weight.1, f32[1,256]{1,0:T(1,128)} %bitcast.10, ...), custom_call_target="tpu_custom_call" | custom-call | tf_op jit(solution)/shard_map/pallas_call | solution.py:377
  50.0 1.7 %shard_map.122 = (bf16[256,256]{1,0:T(8,128)(2,1)}, f32[128,256]{1,0:T(8,128)}, f32[1,256]{1,0:T(1,128)}, bf16[256,128]{1,0:T(8,128)(2,1)}) custom-call(bf16[256,256]{1,0:T(8,128)(2,1)} %get-tuple-element.12.refs_0_, f32[128,256]{1,0:T(8,128)} %get-tuple-element.13.refs_1_, f32[1,256]{1,0:T(1,128)} %get-tuple-element.14.refs_2_, ...), custom_call_target="tpu_custom_call" | custom-call | tf_op jit(solution)/shard_map/pallas_call | solution.py:359
